TPU v7x, 32 devices: a whole 2x2x4 slice. The times are simulated.
32 devices in a mesh: dp: 4 (over x, core), mp: 8 (over z, y).
Axes of the slice: x: 2, y: 2, z: 4, core: 2. Of those that a mesh axis runs over, the one named last changes fastest.
Arguments:
- fast_in: bfloat16 [8, 64, 196, 128], P('dp', 'mp'), may hold values from -6 to 6
- slow_in: bfloat16 [8, 16, 196, 1024], P('dp', 'mp'), may hold values from -6 to 6
- clip_len: int32 [8, 1], replicated, may hold values from 4 to 16, as said below
- w_fast_a: bfloat16 [3, 128, 32], replicated, may hold values from -0.3125 to 0.3125
- w_fast_b: bfloat16 [9, 32, 32], replicated, may hold values from -0.375 to 0.375
- w_fast_c: bfloat16 [32, 128], replicated, may hold values from -1 to 1
- w_lateral: bfloat16 [5, 128, 256], replicated, may hold values from -0.25 to 0.25
- w_slow_a: bfloat16 [3, 1280, 256], P(None, None, 'mp'), may hold values from -0.09375 to 0.09375
- w_slow_b: bfloat16 [9, 256, 256], P(None, None, 'mp'), may hold values from -0.125 to 0.125
- w_slow_c: bfloat16 [256, 1024], P(None, 'mp'), may hold values from -0.375 to 0.375
- w_short: bfloat16 [1280, 1024], P(None, 'mp'), may hold values from -0.15625 to 0.15625
- norm_fast_a: float32 [2, 32], replicated, may hold values from 0.25 to 1.75
- norm_fast_b: float32 [2, 32], replicated, may hold values from 0.25 to 1.75
- norm_fast_c: float32 [2, 128], replicated, may hold values from 0.25 to 1.75
- norm_slow_a: float32 [2, 256], replicated, may hold values from 0.25 to 1.75
- norm_slow_b: float32 [2, 256], replicated, may hold values from 0.25 to 1.75
- norm_slow_c: float32 [2, 1024], replicated, may hold values from 0.25 to 1.75
- norm_short: float32 [2, 1024], replicated, may hold values from 0.25 to 1.75
- cot_fast: bfloat16 [8, 64, 196, 128], P('dp', 'mp'), may hold values from -6 to 6
- cot_slow: bfloat16 [8, 16, 196, 1024], P('dp', 'mp'), may hold values from -6 to 6
Outputs:
- fast_out: bfloat16 [8, 64, 196, 128], P('dp', 'mp')
- slow_out: bfloat16 [8, 16, 196, 1024], P('dp', 'mp')
- grad_fast_in: bfloat16 [8, 64, 196, 128], P('dp', 'mp')
- grad_slow_in: bfloat16 [8, 16, 196, 1024], P('dp', 'mp')
- grad_w_fast_a: float32 [3, 128, 32], replicated
- grad_w_fast_b: float32 [9, 32, 32], replicated
- grad_w_fast_c: float32 [32, 128], replicated
- grad_w_lateral: float32 [5, 128, 256], replicated
- grad_w_slow_a: float32 [3, 1280, 256], P(None, None, 'mp')
- grad_w_slow_b: float32 [9, 256, 256], P(None, None, 'mp')
- grad_w_slow_c: float32 [256, 1024], P(None, 'mp')
- grad_w_short: float32 [1280, 1024], P(None, 'mp')
- grad_norm_fast_a: float32 [2, 32], replicated
- grad_norm_fast_b: float32 [2, 32], replicated
- grad_norm_fast_c: float32 [2, 128], replicated
- grad_norm_slow_a: float32 [2, 256], replicated
- grad_norm_slow_b: float32 [2, 256], replicated
- grad_norm_slow_c: float32 [2, 1024], replicated
- grad_norm_short: float32 [2, 1024], replicated
Inputs may be any that keep to these rules, and one draw needn't show every extreme that they name: `clip_len`: in every aligned block of 2 rows one row has all 16 slow frames valid.
All inputs are finite; a program needn't handle non-finite values.
Results may differ from a plain program's by a relative error of at most 0.019.
Values may be sent and summed in bfloat16 or wider, within the bound.
No kernel may reach another device: no remote copies, remote signals or barrier semaphores. Data moves between devices by JAX's collectives and lax.ppermute only.
A program may use at most 192 MiB of HBM per device.

v0:
```python
import jax
import jax.numpy as jnp
from jax import lax
from jax.sharding import PartitionSpec as P

H = 14
W = 14
ALPHA = 4


NORM_EPSILON = 1e-05


def padded_2(cells, sides, width):
    for axis, dim in sides:
        count = lax.axis_size(axis)
        ends = count - 1
        head = lax.slice_in_dim(cells, 0, width, axis=dim)
        tail = lax.slice_in_dim(cells, cells.shape[dim] - width, cells.shape[dim], axis=dim)
        cells = jnp.concatenate(
            [
                lax.ppermute(tail, axis, [(i, (i + 1) % count) for i in range(ends)]),
                cells,
                lax.ppermute(head, axis, [((i + 1) % count, i) for i in range(ends)]),
            ],
            axis=dim,
        )
    return cells


def silu_slope(values):
    sigmoid_value = jax.nn.sigmoid(values)
    return sigmoid_value * (1.0 + values * (1.0 - sigmoid_value))


def matmul(left_side, right_side):
    return jnp.dot(left_side, right_side, preferred_element_type=jnp.float32)


def outer_sum(left_side, right_side):
    return jnp.einsum("abpc,abpd->cd", left_side, right_side, preferred_element_type=jnp.float32)


def back_product(upstream, weights):
    return jnp.einsum("abpd,cd->abpc", upstream, weights, preferred_element_type=jnp.float32)


def norm_forward(values, frame_mask, total_count, affine):
    masked = frame_mask[:, :, None, None] * values
    totals, squares = lax.psum(
        (jnp.sum(masked, axis=(0, 1, 2)), jnp.sum(masked * values, axis=(0, 1, 2))), ("dp", "mp")
    )
    average = totals / total_count
    inverse_std = lax.rsqrt(squares / total_count - average * average + NORM_EPSILON)
    standard = (values - average) * inverse_std
    return (affine[0] * standard + affine[1], standard, inverse_std)


def norm_backward(grad_norm_out, standard, inverse_std, frame_mask, total_count, affine):
    grad_beta, grad_gamma = lax.psum(
        (jnp.sum(grad_norm_out, axis=(0, 1, 2)), jnp.sum(grad_norm_out * standard, axis=(0, 1, 2))),
        ("dp", "mp"),
    )
    grad_values = (
        frame_mask[:, :, None, None]
        * (inverse_std * affine[0])
        * (grad_norm_out - (grad_beta + standard * grad_gamma) / total_count)
    )
    return (grad_values, jnp.stack([grad_gamma, grad_beta]))


def spatial_patches(inputs):
    leading, frames_here, pixels, channels = inputs.shape
    padded_grid = jnp.pad(
        inputs.reshape(leading * frames_here, H, W, channels), ((0, 0), (1, 1), (1, 1), (0, 0))
    )
    pieces = [
        padded_grid[:, row_shift : row_shift + H, col_shift : col_shift + W]
        for row_shift in range(3)
        for col_shift in range(3)
    ]
    return jnp.concatenate(pieces, -1).reshape(leading, frames_here, pixels, 9 * channels)


def spatial_fold(upstream):
    leading, frames_here, pixels, widths = upstream.shape
    channels = widths // 9
    pieces = upstream.reshape(leading * frames_here, H, W, 9, channels)
    running = jnp.zeros((leading * frames_here, H + 2, W + 2, channels), jnp.float32)
    for row_shift in range(3):
        for col_shift in range(3):
            running = running + jnp.pad(
                pieces[:, :, :, 3 * row_shift + col_shift],
                ((0, 0), (row_shift, 2 - row_shift), (col_shift, 2 - col_shift), (0, 0)),
            )
    return running[:, 1 : H + 1, 1 : W + 1].reshape(leading, frames_here, pixels, channels)


def frame_stack(padded, frames_here, tap_count):
    return jnp.concatenate(
        [padded[:, offset : offset + frames_here] for offset in range(tap_count)], -1
    )


def frame_fold(upstream, tap_count):
    channels = upstream.shape[-1] // tap_count
    running = jnp.pad(upstream[..., :channels], ((0, 0), (0, tap_count - 1), (0, 0), (0, 0)))
    for offset in range(1, tap_count):
        running = running + jnp.pad(
            upstream[..., offset * channels : (offset + 1) * channels],
            ((0, 0), (offset, tap_count - 1 - offset), (0, 0), (0, 0)),
        )
    return running


def lateral_fold(upstream):
    channels = upstream.shape[-1] // 5
    parts = [upstream[..., offset * channels : (offset + 1) * channels] for offset in range(5)]
    after = ((0, 0), (0, 1), (0, 0), (0, 0))
    before = ((0, 0), (1, 0), (0, 0), (0, 0))
    leading_slot = jnp.pad(parts[0], after) + jnp.pad(parts[4], before)
    stacked = jnp.stack(
        [leading_slot] + [jnp.pad(parts[offset], after) for offset in range(1, 4)], 2
    )
    return stacked.reshape(stacked.shape[0], -1, stacked.shape[3], channels)


def per_device(
    fast_in,
    slow_in,
    clip_len,
    w_fast_a,
    w_fast_b,
    w_fast_c,
    w_lateral,
    w_slow_a,
    w_slow_b,
    w_slow_c,
    w_short,
    norm_fast_a,
    norm_fast_b,
    norm_fast_c,
    norm_slow_a,
    norm_slow_b,
    norm_slow_c,
    norm_short,
    cot_fast,
    cot_slow,
):
    batch_here, fast_frames, pixels, fast_width = fast_in.shape
    slow_frames = slow_in.shape[1]
    slow_width = slow_in.shape[3]
    inner_width = w_fast_a.shape[2]
    lateral_width = w_lateral.shape[2]
    clip_count = clip_len.shape[1]
    slot_fast = fast_frames * lax.axis_size("mp") // clip_count
    slot_slow = slot_fast // ALPHA
    rows_here = lax.dynamic_slice_in_dim(clip_len, lax.axis_index("dp") * batch_here, batch_here, 0)
    fast_start = lax.axis_index("mp") * fast_frames
    clip_here = fast_start // slot_fast
    length_here = jnp.sum(
        jnp.where(jnp.arange(clip_count)[None, :] == clip_here, rows_here, 0), axis=1
    )
    fast_mask = (
        (fast_start % slot_fast + jnp.arange(fast_frames))[None, :] < ALPHA * length_here[:, None]
    ).astype(jnp.float32)
    slow_start = lax.axis_index("mp") * slow_frames
    slow_mask = (
        (slow_start % slot_slow + jnp.arange(slow_frames))[None, :] < length_here[:, None]
    ).astype(jnp.float32)
    fast_count = jnp.sum(clip_len).astype(jnp.float32) * (ALPHA * pixels)
    slow_count = jnp.sum(clip_len).astype(jnp.float32) * pixels
    keep_lower = (fast_start % slot_fast != 0).astype(jnp.float32)
    keep_upper = ((fast_start + fast_frames) % slot_fast != 0).astype(jnp.float32)
    lower_bf = keep_lower.astype(jnp.bfloat16)
    upper_bf = keep_upper.astype(jnp.bfloat16)
    fast_keep = fast_mask[:, :, None, None]
    slow_keep = slow_mask[:, :, None, None]
    fast_masked = fast_in * fast_keep.astype(jnp.bfloat16)
    padded_fast = padded_2(fast_masked, (("mp", 1),), 2)
    padded_fast = jnp.concatenate(
        [padded_fast[:, :2] * lower_bf, padded_fast[:, 2:-2], padded_fast[:, -2:] * upper_bf], 1
    )
    fast_stack = frame_stack(padded_fast[:, 1:-1], fast_frames, 3)
    fast_first = matmul(fast_stack, w_fast_a.reshape(-1, inner_width))
    norm_fa, standard_fa, inverse_fa = norm_forward(fast_first, fast_mask, fast_count, norm_fast_a)
    hidden_a = (fast_keep * jax.nn.silu(norm_fa)).astype(jnp.bfloat16)
    patches_a = spatial_patches(hidden_a)
    fast_second = matmul(patches_a, w_fast_b.reshape(-1, inner_width))
    norm_fb, standard_fb, inverse_fb = norm_forward(fast_second, fast_mask, fast_count, norm_fast_b)
    hidden_b = (fast_keep * jax.nn.silu(norm_fb)).astype(jnp.bfloat16)
    fast_third = matmul(hidden_b, w_fast_c)
    norm_fc, standard_fc, inverse_fc = norm_forward(fast_third, fast_mask, fast_count, norm_fast_c)
    fast_sum = norm_fc + fast_masked.astype(jnp.float32)
    fast_out = (fast_keep * jax.nn.silu(fast_sum)).astype(jnp.bfloat16)
    lateral_stack = jnp.concatenate(
        [padded_fast[:, offset : offset + 4 * slow_frames : 4] for offset in range(5)], -1
    )
    lateral_out = matmul(lateral_stack, w_lateral.reshape(-1, lateral_width)).astype(jnp.bfloat16)
    joined = jnp.concatenate([slow_in, lateral_out], -1) * slow_keep.astype(jnp.bfloat16)
    padded_slow = padded_2(joined, (("mp", 1),), 1)
    padded_slow = jnp.concatenate(
        [padded_slow[:, :1] * lower_bf, padded_slow[:, 1:-1], padded_slow[:, -1:] * upper_bf], 1
    )
    full_a, full_b, full_c, full_short = (
        lax.all_gather(w_slow_a, "mp", axis=2, tiled=True),
        lax.all_gather(w_slow_b, "mp", axis=2, tiled=True),
        lax.all_gather(w_slow_c, "mp", axis=1, tiled=True),
        lax.all_gather(w_short, "mp", axis=1, tiled=True),
    )
    middle_width = full_a.shape[2]
    slow_stack = frame_stack(padded_slow, slow_frames, 3)
    slow_first = matmul(slow_stack, full_a.reshape(-1, middle_width))
    norm_sa, standard_sa, inverse_sa = norm_forward(slow_first, slow_mask, slow_count, norm_slow_a)
    hidden_c = (slow_keep * jax.nn.silu(norm_sa)).astype(jnp.bfloat16)
    patches_c = spatial_patches(hidden_c)
    slow_second = matmul(patches_c, full_b.reshape(-1, middle_width))
    norm_sb, standard_sb, inverse_sb = norm_forward(slow_second, slow_mask, slow_count, norm_slow_b)
    hidden_d = (slow_keep * jax.nn.silu(norm_sb)).astype(jnp.bfloat16)
    slow_third = matmul(hidden_d, full_c)
    shortcut = matmul(joined, full_short)
    norm_sc, standard_sc, inverse_sc = norm_forward(slow_third, slow_mask, slow_count, norm_slow_c)
    norm_sh, standard_sh, inverse_sh = norm_forward(shortcut, slow_mask, slow_count, norm_short)
    slow_sum = norm_sc + norm_sh
    slow_out = (slow_keep * jax.nn.silu(slow_sum)).astype(jnp.bfloat16)
    back_a, back_b, back_c, back_short = (full_a, full_b, full_c, full_short)
    slow_cot = cot_slow.astype(jnp.float32) * slow_keep * silu_slope(slow_sum)
    d_slow_third, grad_norm_slow_c = norm_backward(
        slow_cot, standard_sc, inverse_sc, slow_mask, slow_count, norm_slow_c
    )
    d_shortcut, grad_norm_short = norm_backward(
        slow_cot, standard_sh, inverse_sh, slow_mask, slow_count, norm_short
    )
    d_third_low = d_slow_third.astype(jnp.bfloat16)
    d_short_low = d_shortcut.astype(jnp.bfloat16)
    slow_grad_c = outer_sum(hidden_d, d_third_low)
    slow_grad_short = outer_sum(joined, d_short_low)
    d_hidden_d = back_product(d_third_low, back_c)
    d_slow_second, grad_norm_slow_b = norm_backward(
        d_hidden_d * slow_keep * silu_slope(norm_sb),
        standard_sb,
        inverse_sb,
        slow_mask,
        slow_count,
        norm_slow_b,
    )
    d_second_low = d_slow_second.astype(jnp.bfloat16)
    slow_grad_b = outer_sum(patches_c, d_second_low).reshape(9, middle_width, middle_width)
    d_hidden_c = spatial_fold(back_product(d_second_low, back_b.reshape(-1, middle_width)))
    d_slow_first, grad_norm_slow_a = norm_backward(
        d_hidden_c * slow_keep * silu_slope(norm_sa),
        standard_sa,
        inverse_sa,
        slow_mask,
        slow_count,
        norm_slow_a,
    )
    d_first_low = d_slow_first.astype(jnp.bfloat16)
    slow_grad_a = outer_sum(slow_stack, d_first_low).reshape(3, -1, middle_width)
    d_padded_slow = frame_fold(back_product(d_first_low, back_a.reshape(-1, middle_width)), 3)
    slow_rims = jnp.concatenate(
        [d_padded_slow[:, :1] * keep_lower, d_padded_slow[:, -1:] * keep_upper], 1
    )
    slow_back = padded_2(slow_rims.astype(jnp.bfloat16), (("mp", 1),), 1).astype(slow_rims.dtype)
    slow_edges = jnp.pad(
        slow_back[:, :1], ((0, 0), (0, slow_frames - 1), (0, 0), (0, 0))
    ) + jnp.pad(slow_back[:, -1:], ((0, 0), (slow_frames - 1, 0), (0, 0), (0, 0)))
    d_joined = slow_keep * (
        d_padded_slow[:, 1:-1] + slow_edges + back_product(d_short_low, back_short)
    )
    grad_slow_in = d_joined[..., :slow_width].astype(jnp.bfloat16)
    d_lateral_low = d_joined[..., slow_width:].astype(jnp.bfloat16)
    fast_grad_lateral = outer_sum(lateral_stack, d_lateral_low)
    d_padded_fast = lateral_fold(back_product(d_lateral_low, w_lateral.reshape(-1, lateral_width)))
    fast_cot = cot_fast.astype(jnp.float32) * fast_keep * silu_slope(fast_sum)
    d_fast_third, grad_norm_fast_c = norm_backward(
        fast_cot, standard_fc, inverse_fc, fast_mask, fast_count, norm_fast_c
    )
    d_fthird_low = d_fast_third.astype(jnp.bfloat16)
    fast_grad_c = outer_sum(hidden_b, d_fthird_low)
    d_hidden_b = back_product(d_fthird_low, w_fast_c)
    d_fast_second, grad_norm_fast_b = norm_backward(
        d_hidden_b * fast_keep * silu_slope(norm_fb),
        standard_fb,
        inverse_fb,
        fast_mask,
        fast_count,
        norm_fast_b,
    )
    d_fsecond_low = d_fast_second.astype(jnp.bfloat16)
    fast_grad_b = outer_sum(patches_a, d_fsecond_low)
    d_hidden_a = spatial_fold(back_product(d_fsecond_low, w_fast_b.reshape(-1, inner_width)))
    d_fast_first, grad_norm_fast_a = norm_backward(
        d_hidden_a * fast_keep * silu_slope(norm_fa),
        standard_fa,
        inverse_fa,
        fast_mask,
        fast_count,
        norm_fast_a,
    )
    d_ffirst_low = d_fast_first.astype(jnp.bfloat16)
    fast_grad_a = outer_sum(fast_stack, d_ffirst_low)
    d_inner = frame_fold(back_product(d_ffirst_low, w_fast_a.reshape(-1, inner_width)), 3)
    d_padded_fast = d_padded_fast + jnp.pad(d_inner, ((0, 0), (1, 1), (0, 0), (0, 0)))
    fast_rims = jnp.concatenate(
        [d_padded_fast[:, :2] * keep_lower, d_padded_fast[:, -2:] * keep_upper], 1
    )
    fast_back = padded_2(fast_rims.astype(jnp.bfloat16), (("mp", 1),), 2).astype(fast_rims.dtype)
    fast_edges = jnp.pad(
        fast_back[:, :2], ((0, 0), (0, fast_frames - 2), (0, 0), (0, 0))
    ) + jnp.pad(fast_back[:, -2:], ((0, 0), (fast_frames - 2, 0), (0, 0), (0, 0)))
    grad_fast_in = (fast_keep * (d_padded_fast[:, 2:-2] + fast_edges + fast_cot)).astype(
        jnp.bfloat16
    )
    summed_a, summed_b, summed_c, summed_lateral = lax.psum(
        (fast_grad_a, fast_grad_b, fast_grad_c, fast_grad_lateral), ("dp", "mp")
    )
    whole = (
        lax.psum(slow_grad_a.astype(jnp.bfloat16), "dp").astype(jnp.float32),
        lax.psum(slow_grad_b.astype(jnp.bfloat16), "dp").astype(jnp.float32),
        lax.psum(slow_grad_c.astype(jnp.bfloat16), "dp").astype(jnp.float32),
        lax.psum(slow_grad_short.astype(jnp.bfloat16), "dp").astype(jnp.float32),
    )
    pieces = (
        lax.psum_scatter(
            whole[0].astype(jnp.bfloat16), "mp", scatter_dimension=2, tiled=True
        ).astype(jnp.float32),
        lax.psum_scatter(
            whole[1].astype(jnp.bfloat16), "mp", scatter_dimension=2, tiled=True
        ).astype(jnp.float32),
        lax.psum_scatter(
            whole[2].astype(jnp.bfloat16), "mp", scatter_dimension=1, tiled=True
        ).astype(jnp.float32),
        lax.psum_scatter(
            whole[3].astype(jnp.bfloat16), "mp", scatter_dimension=1, tiled=True
        ).astype(jnp.float32),
    )
    return (
        fast_out,
        slow_out,
        grad_fast_in,
        grad_slow_in,
        summed_a.reshape(3, fast_width, inner_width),
        summed_b.reshape(9, inner_width, inner_width),
        summed_c,
        summed_lateral.reshape(5, fast_width, lateral_width),
        pieces[0],
        pieces[1],
        pieces[2],
        pieces[3],
        grad_norm_fast_a,
        grad_norm_fast_b,
        grad_norm_fast_c,
        grad_norm_slow_a,
        grad_norm_slow_b,
        grad_norm_slow_c,
        grad_norm_short,
    )


def solution(mesh):
    placed = (
        P("dp", "mp", None, None),
        P("dp", "mp", None, None),
        P(),
        P(),
        P(),
        P(),
        P(),
        P(None, None, "mp"),
        P(None, None, "mp"),
        P(None, "mp"),
        P(None, "mp"),
        P(),
        P(),
        P(),
        P(),
        P(),
        P(),
        P(),
        P("dp", "mp", None, None),
        P("dp", "mp", None, None),
    )
    return jax.shard_map(
        per_device,
        mesh=mesh,
        in_specs=placed,
        out_specs=(
            P("dp", "mp", None, None),
            P("dp", "mp", None, None),
            P("dp", "mp", None, None),
            P("dp", "mp", None, None),
            P(),
            P(),
            P(),
            P(),
            P(None, None, "mp"),
            P(None, None, "mp"),
            P(None, "mp"),
            P(None, "mp"),
            P(),
            P(),
            P(),
            P(),
            P(),
            P(),
            P(),
        ),
        check_vma=False,
    )
```

profile of v0, /device:TPU:0, one launch (start us, length us, event | category | flops | bytes accessed | tf_op | source)
XLA Modules:
  0.0 1118.2 jit_solution(8175187924515476513)
XLA Ops:
  11.0 5.6 collective-permute-start
  22.4 31.7 %all_gather.14 = bf16[256,1024]{1,0:T(8,128)(2,1)} all-gather(bf16[256,128]{1,0:T(8,128)(2,1)S(1)} %copy-done.54), channel_id=1, replica_groups=mesh['dp'=4,'mp'=8] {'mp'}, dimensions={1}, use_global_device_ids=true | all-gather | bytes 589824 | tf_op jit(solution)/shard_map/all_gather | solution.py:208
  61.1 40.4 %all-reduce.40 = (f32[32]{0:T(128)}, f32[32]{0:T(128)}) all-reduce(f32[32]{0:T(128)} %get-tuple-element.117, f32[32]{0:T(128)} %get-tuple-element.116), channel_id=1, replica_groups=mesh['dp'=4,'mp'=8] {'dp','mp'}, use_global_device_ids=true, to_apply=%region_1.2 | all-reduce | flops 64 | bytes 512 | tf_op jit(solution)/shard_map/psum | solution.py:50
  105.0 2.5 copy.199
  118.1 6.2 collective-permute-start.2
  124.3 2.3 pad_slice_fusion
  126.7 2.5 copy.201
  129.1 2.5 copy.202
  131.6 2.5 copy.203
  134.0 2.5 copy.204
  147.0 2.5 copy.207
  154.0 24.6 %collective-permute-done.2 = bf16[2,1,196,1280]{3,0,2,1:T(2,128)(2,1)} collective-permute-done((bf16[2,1,196,1280]{3,0,2,1:T(2,128)(2,1)}, bf16[2,1,196,1280]{3,0,2,1:T(2,128)(2,1)}, u32[]{:S(2)}, u32[]{:S(2)}) %collective-permute-start.2) | collective-permute-done | bytes 1003552 | tf_op jit(solution)/shard_map/ppermute | solution.py:22
  181.1 2.4 copy.224
  183.5 4.0 copy.214
  187.4 5.5 fusion.26
  192.9 42.5 %all-reduce.39 = (f32[32]{0:T(128)S(1)}, f32[32]{0:T(128)}, f32[256]{0:T(256)S(1)}, f32[256]{0:T(256)S(1)}) all-reduce(f32[32]{0:T(128)S(1)} %copy-done.126, f32[32]{0:T(128)S(1)} %copy-done.125, f32[256]{0:T(256)S(1)} %get-tuple-element.109, f32[256]{0:T(256)S(1)} %get-tuple-element.108), channel_id=1, replica_groups=mesh['dp'=4,'mp'=8] {'dp','mp'}, use_global_device_ids=true, to_apply=%region_6.7 | all-reduce | flops 576 | bytes 4608 | tf_op jit(solution)/shard_map/psum | solution.py:50
  236.2 2.2 pad_slice_fusion.8
  257.9 41.6 %all-reduce.38 = (f32[128]{0:T(128)S(1)}, f32[128]{0:T(128)S(1)}, f32[256]{0:T(256)S(1)}, f32[256]{0:T(256)S(1)}) all-reduce(f32[128]{0:T(128)S(1)} %get-tuple-element.103, f32[128]{0:T(128)S(1)} %get-tuple-element.102, f32[256]{0:T(256)S(1)} %get-tuple-element.107, ...), channel_id=1, replica_groups=mesh['dp'=4,'mp'=8] {'dp','mp'}, use_global_device_ids=true, to_apply=%region_10.11 | all-reduce | flops 768 | bytes 6144 | tf_op jit(solution)/shard_map/psum | solution.py:50
  301.6 4.7 fusion.67
  306.3 5.3 fusion.11
  311.6 3.5 multiply_reduce_fusion.1
  315.2 39.5 %all-reduce.37 = (f32[1024]{0:T(1024)}, f32[1024]{0:T(1024)}, f32[1024]{0:T(1024)}, f32[1024]{0:T(1024)}, f32[128]{0:T(128)}, /*index=5*/f32[128]{0:T(128)}) all-reduce(f32[1024]{0:T(1024)} %get-tuple-element.122, f32[1024]{0:T(1024)} %get-tuple-element.123, ...), channel_id=1, replica_groups=mesh['dp'=4,'mp'=8] {'dp','mp'}, use_global_device_ids=true, to_apply=%region_28.29 | all-reduce | flops 4352 | bytes 34816 | tf_op jit(solution)/shard_map/psum | solution.py:50
  361.7 5.0 multiply_reduce_fusion.2
  366.7 42.3 %all-reduce.36 = (f32[1024]{0:T(1024)}, f32[1024]{0:T(1024)S(1)}, f32[32]{0:T(128)}, f32[32]{0:T(128)}) all-reduce(f32[1024]{0:T(1024)} %get-tuple-element.100, f32[1024]{0:T(1024)} %get-tuple-element.101, f32[32]{0:T(128)} %get-tuple-element.121, f32[32]{0:T(128)} %get-tuple-element.120), channel_id=1, replica_groups=mesh['dp'=4,'mp'=8] {'dp','mp'}, use_global_device_ids=true, to_apply=%region_32.33 | all-reduce | flops 2112 | bytes 16896 | tf_op jit(solution)/shard_map/psum | solution.py:60
  411.1 3.1 fusion.84
  414.2 2.5 copy.244
  418.2 3.9 multiply_convert_fusion.1
  422.2 2.4 fusion.69
  424.6 7.1 fusion.47
  431.7 10.6 slice_bitcast_fusion.8
  442.3 2.9 pad_add_fusion.2
  446.6 4.0 pad_add_fusion.4
  450.6 2.9 copy.253
  453.4 2.8 fusion.70
  456.3 39.5 %all-reduce.35 = (f32[256]{0:T(256)}, f32[256]{0:T(256)}, f32[32]{0:T(128)}, f32[32]{0:T(128)}) all-reduce(f32[256]{0:T(256)} %get-tuple-element.113, f32[256]{0:T(256)} %get-tuple-element.112, f32[32]{0:T(128)} %get-tuple-element.119, f32[32]{0:T(128)} %get-tuple-element.118), channel_id=1, replica_groups=mesh['dp'=4,'mp'=8] {'dp','mp'}, use_global_device_ids=true, to_apply=%region_36.37 | all-reduce | flops 576 | bytes 4608 | tf_op jit(solution)/shard_map/psum | solution.py:60
  500.6 2.4 multiply_convert_fusion.6
  504.1 2.5 fusion.24
  512.3 3.1 fusion.68
  515.5 2.5 fusion.22
  519.1 124.8 %all-reduce.48.cloned.1.call-done = (f32[256]{0:T(256)}, f32[256]{0:T(256)}, f32[1024]{0:T(1024)}, f32[3,128,32]{1,0,2:T(4,128)}, f32[9,32,32]{2,1,0:T(8,128)}, /*index=5*/f32[32,128]{1,0:T(8,128)}) async-done(((f32[256]{0:T(256)}, f32[256]{0:T(256)}, f32[1024]{0:T(1024)}, f32[3,128,32]{1,0,2:T(4,128)}, f32[9,32,32]{2,1,0:T(8,128)}, /*index=5*/f32[32,128]{1,0:T(8,128)}), (f32[256]{0:T(256)}, f32[256]{0:T(256)}, ...) | async-done | bytes 108560 | tf_op jit(solution)/shard_map/psum | solution.py:60
  643.9 4.0 multiply_convert_fusion
  649.1 4.2 bitcast_convert_fusion
  653.3 4.4 copy.292
  658.1 6.4 copy.256
  666.7 2.8 copy.259
  675.1 2.5 bitcast_convert_fusion.1
  677.7 3.5 pad_add_fusion.3
  682.7 6.3 fusion.83
  689.0 8.8 fusion.74
  697.8 3.5 fusion.16
  705.3 5.5 collective-permute-start.4
  710.8 5.7 fusion.2
  716.5 4.0 copy.255
  722.6 7.9 pad_add_fusion
  735.0 23.7 %collective-permute-done.4 = bf16[2,1,196,1280]{3,0,2,1:T(2,128)(2,1)} collective-permute-done((bf16[2,1,196,1280]{3,0,2,1:T(2,128)(2,1)S(1)}, bf16[2,1,196,1280]{3,0,2,1:T(2,128)(2,1)}, u32[]{:S(2)}, u32[]{:S(2)}) %collective-permute-start.4) | collective-permute-done | bytes 1003552 | tf_op jit(solution)/shard_map/ppermute | solution.py:22
  764.8 2.5 fusion.7
  770.9 27.9 %reduce-scatter.15.cloned.1.call-done = bf16[128,1280]{1,0:T(8,128)(2,1)} async-done(((bf16[1024,1280]{1,0:T(8,128)(2,1)}), bf16[128,1280]{1,0:T(8,128)(2,1)}) %reduce-scatter.15.cloned.1.call-update) | async-done | bytes 327696
  800.7 66.0 %reduce-scatter.11.cloned.1.call-done = bf16[9,256,32]{1,2,0:T(8,128)(2,1)} async-done(((bf16[9,256,256]{1,2,0:T(8,128)(2,1)}), bf16[9,256,32]{1,2,0:T(8,128)(2,1)}) %reduce-scatter.11.cloned.1.call-update) | async-done | bytes 147472 | tf_op jit(solution)/shard_map/reduce_scatter | solution.py:328
  866.7 69.7 %reduce-scatter.9.cloned.1.call-done = bf16[3,1280,32]{1,2,0:T(8,128)(2,1)} async-done(((bf16[3,1280,256]{1,2,0:T(8,128)(2,1)}), bf16[3,1280,32]{1,2,0:T(8,128)(2,1)}) %reduce-scatter.9.cloned.1.call-update) | async-done | bytes 245776 | tf_op jit(solution)/shard_map/reduce_scatter | solution.py:325
  937.9 2.8 copy.261
  940.7 2.6 collective-permute-start.6
  946.1 2.7 collective-permute-done.6
  954.1 19.3 %all-reduce.50.cloned.1.call-done = (bf16[3,1280,32]{1,2,0:T(8,128)(2,1)}, bf16[9,256,32]{1,2,0:T(8,128)(2,1)}, bf16[256,128]{1,0:T(8,128)(2,1)}, bf16[1280,128]{1,0:T(8,128)(2,1)}) async-done(((bf16[3,1280,32]{1,2,0:T(8,128)(2,1)}, bf16[9,256,32]{1,2,0:T(8,128)(2,1)}, bf16[256,128]{1,0:T(8,128)(2,1)}, bf16[1280,128]{1,0:T(8,128)(2,1)}), (bf16[3,1280,32]{1,2,0:T(8,128)(2,1)}, bf16[9,256,32]{1,2,0:T(8,128)(2,1)}, ...) | async-done | bytes 786448 | tf_op jit(solution)/shard_map/psum | solution.py:319
  980.1 127.8 %all-reduce.46.cloned.1.call-done = f32[5,128,256]{2,1,0:T(8,128)} async-done(((f32[5,128,256]{2,1,0:T(8,128)}), f32[5,128,256]{2,1,0:T(8,128)}) %all-reduce.46.cloned.1.call-update) | async-done | bytes 655376 | tf_op jit(solution)/shard_map/psum | solution.py:315
  (471 shorter events, 145.5 us)
Async XLA Ops:
  7.2 104.4 %copy-start = (bf16[5,128,256]{2,1,0:T(8,128)(2,1)S(1)}, bf16[5,128,256]{2,1,0:T(8,128)(2,1)}, u32[]{:S(2)}) copy-start(bf16[5,128,256]{2,1,0:T(8,128)(2,1)} %param.26) | copy-start | bytes 983044
  7.2 10.8 copy-start.136
  7.2 12.1 %copy-start.111 = (f32[2,32]{1,0:T(2,128)S(1)}, f32[2,32]{1,0:T(2,128)}, u32[]{:S(2)}) copy-start(f32[2,32]{1,0:T(2,128)} %param.31) | copy-start | bytes 772
  7.2 12.7 %copy-start.112 = (f32[2,32]{1,0:T(2,128)S(1)}, f32[2,32]{1,0:T(2,128)}, u32[]{:S(2)}) copy-start(f32[2,32]{1,0:T(2,128)} %param.32) | copy-start | bytes 772
  7.2 13.2 %copy-start.128 = (f32[2,256]{1,0:T(2,128)S(1)}, f32[2,256]{1,0:T(2,128)}, u32[]{:S(2)}) copy-start(f32[2,256]{1,0:T(2,128)} %param.34) | copy-start | bytes 6148
  7.3 13.2 %copy-start.129 = (f32[2,256]{1,0:T(2,128)S(1)}, f32[2,256]{1,0:T(2,128)}, u32[]{:S(2)}) copy-start(f32[2,256]{1,0:T(2,128)} %param.35) | copy-start | bytes 6148
  7.3 13.8 %copy-start.84 = (f32[2,1024]{1,0:T(2,128)S(1)}, f32[2,1024]{1,0:T(2,128)}, u32[]{:S(2)}) copy-start(f32[2,1024]{1,0:T(2,128)} %param.36) | copy-start | bytes 24580
  7.3 14.4 %copy-start.85 = (f32[2,1024]{1,0:T(2,128)S(1)}, f32[2,1024]{1,0:T(2,128)}, u32[]{:S(2)}) copy-start(f32[2,1024]{1,0:T(2,128)} %param.37) | copy-start | bytes 24580
  7.3 15.0 %copy-start.68 = (bf16[3,128,32]{1,2,0:T(8,128)(2,1)S(1)}, bf16[3,128,32]{1,2,0:T(8,128)(2,1)}, u32[]{:S(2)}) copy-start(bf16[3,128,32]{1,2,0:T(8,128)(2,1)} %param.23) | copy-start | bytes 73732
  7.3 15.1 %copy-start.54 = (bf16[256,128]{1,0:T(8,128)(2,1)S(1)}, bf16[256,128]{1,0:T(8,128)(2,1)}, u32[]{:S(2)}) copy-start(bf16[256,128]{1,0:T(8,128)(2,1)} %param.29) | copy-start | bytes 196612
  7.3 173.8 %all-gather.6.cloned.1.call-start = ((), (), s32[]{:S(2)}) async-start(), calls=%async_computation.5 | async-start | bytes 1327104 | tf_op jit(solution)/shard_map/all_gather | solution.py:207
  8.0 175.4 %all-gather.4.cloned.1.call-start = ((), (), s32[]{:S(2)}) async-start(), calls=%async_computation.4 | async-start | bytes 2211840 | tf_op jit(solution)/shard_map/all_gather | solution.py:206
  8.8 297.5 %all-gather.8.cloned.1.call-start = ((), (), s32[]{:S(2)}) async-start(), calls=%async_computation.6 | async-start | bytes 2949120 | tf_op jit(solution)/shard_map/all_gather | solution.py:209
  9.7 46.2 %copy-start.86 = (bf16[2,8]{1,0:T(2,128)(2,1)}, bf16[2,8]{1,0:T(2,128)(2,1)S(1)}, u32[]{:S(2)}) copy-start(bf16[2,8]{1,0:T(2,128)(2,1)S(1)} %get-tuple-element.262) | copy-start | bytes 100
  11.0 98.5 %copy-start.20 = (bf16[2,8,196,128]{3,2,1,0:T(8,128)(2,1)}, bf16[2,8,196,128]{3,2,1,0:T(8,128)(2,1)S(1)}, u32[]{:S(2)}) copy-start(bf16[2,8,196,128]{3,2,1,0:T(8,128)(2,1)S(1)} %copy_multiply_fusion) | copy-start | bytes 2408452
  11.0 45.5 %copy-start.114 = (f32[2,128]{1,0:T(2,128)S(1)}, f32[2,128]{1,0:T(2,128)}, u32[]{:S(2)}) copy-start(f32[2,128]{1,0:T(2,128)} %param.33) | copy-start | bytes 3076
  11.0 46.0 %collective-permute-start = (bf16[2,2,196,128]{3,2,1,0:T(8,128)(2,1)S(1)}, bf16[2,2,196,128]{3,2,1,0:T(8,128)(2,1)}, u32[]{:S(2)}, u32[]{:S(2)}) collective-permute-start(bf16[2,2,196,128]{3,2,1,0:T(8,128)(2,1)S(1)} %get-tuple-element.214), channel_id=1, source_target_pairs={{0,1},{1,2},{2,3},{3,4},{4,5},{5,6},{6,7},{8,9},{9,10},{10,11},{11... | collective-permute-start | bytes 602120 | tf_op jit(solution)/shard_map/ppermute | solution.py:22
  16.6 41.4 %collective-permute-start.1 = (bf16[2,2,196,128]{3,2,1,0:T(8,128)(2,1)S(1)}, bf16[2,2,196,128]{3,2,1,0:T(8,128)(2,1)S(1)}, u32[]{:S(2)}, u32[]{:S(2)}) collective-permute-start(bf16[2,2,196,128]{3,2,1,0:T(8,128)(2,1)S(1)} %get-tuple-element.215), channel_id=1, source_target_pairs={{1,0},{2,1},{3,2},{4,3},{5,4},{6,5},{7,6},{9,8},{10,9},{11,10},{12... | collective-permute-start | bytes 602120 | tf_op jit(solution)/shard_map/ppermute | solution.py:24
  17.9 626.0 %all-reduce.48.cloned.1.call-start = ((), (), s32[]{:S(2)}) async-start(), calls=%async_computation.12 | async-start | bytes 471040 | tf_op jit(solution)/shard_map/psum | solution.py:60
  20.5 232.2 %copy-start.66 = (f32[1,256]{1,0:T(1,128)}, f32[1,256]{1,0:T(1,128)S(1)}, u32[]{:S(2)}) copy-start(f32[1,256]{1,0:T(1,128)S(1)} %get-tuple-element.246) | copy-start | bytes 3076
  20.5 232.2 %copy-start.76 = (f32[1,256]{1,0:T(1,128)}, f32[1,256]{1,0:T(1,128)S(1)}, u32[]{:S(2)}) copy-start(f32[1,256]{1,0:T(1,128)S(1)} %get-tuple-element.247) | copy-start | bytes 3076
  113.3 11.0 copy-start.23
  116.8 35.8 %collective-permute-start.3 = (bf16[2,1,196,1280]{3,0,2,1:T(2,128)(2,1)}, bf16[2,1,196,1280]{3,0,2,1:T(2,128)(2,1)}, u32[]{:S(2)}, u32[]{:S(2)}) collective-permute-start(bf16[2,1,196,1280]{3,0,2,1:T(2,128)(2,1)} %copy.212), channel_id=1, source_target_pairs={{1,0},{2,1},{3,2},{4,3},{5,4},{6,5},{7,6},{9,8},{10,9},{11,10},{12... | collective-permute-start | bytes 3010568 | tf_op jit(solution)/shard_map/ppermute | solution.py:24
  118.1 60.6 %collective-permute-start.2 = (bf16[2,1,196,1280]{3,0,2,1:T(2,128)(2,1)}, bf16[2,1,196,1280]{3,0,2,1:T(2,128)(2,1)}, u32[]{:S(2)}, u32[]{:S(2)}) collective-permute-start(bf16[2,1,196,1280]{3,0,2,1:T(2,128)(2,1)} %copy.210), channel_id=1, source_target_pairs={{0,1},{1,2},{2,3},{3,4},{4,5},{5,6},{6,7},{8,9},{9,10},{10,11},{11... | collective-permute-start | bytes 3010568 | tf_op jit(solution)/shard_map/ppermute | solution.py:22
  136.5 8.2 copy-start.79
  136.5 8.2 copy-start.81
  136.5 8.2 copy-start.82
  136.5 8.2 copy-start.83
  140.7 6.2 copy-start.41
  142.7 7.7 copy-start.50
  154.0 33.4 %copy-start.42 = (bf16[2,1,196,1280]{3,2,1,0:T(8,128)(2,1)}, bf16[2,1,196,1280]{3,2,1,0:T(8,128)(2,1)S(1)}, u32[]{:S(2)}) copy-start(bf16[2,1,196,1280]{3,2,1,0:T(8,128)(2,1)S(1)} %copy.213) | copy-start | bytes 3010564
  235.5 17.2 %copy-start.62 = (f32[256]{0:T(256)}, f32[256]{0:T(256)S(1)}, u32[]{:S(2)}) copy-start(f32[256]{0:T(256)S(1)} %get-tuple-element.159) | copy-start | bytes 3076
  235.5 17.2 %copy-start.64 = (f32[256]{0:T(256)}, f32[256]{0:T(256)S(1)}, u32[]{:S(2)}) copy-start(f32[256]{0:T(256)S(1)} %get-tuple-element.160) | copy-start | bytes 3076
  255.8 43.7 %copy-start.115 = (f32[2,128]{1,0:T(2,128)S(1)}, f32[2,128]{1,0:T(2,128)}, u32[]{:S(2)}) copy-start(f32[2,128]{1,0:T(2,128)} %param.33) | copy-start | bytes 3076
  255.8 43.7 %copy-start.107 = (f32[1,256]{1,0:T(1,128)S(1)}, f32[1,256]{1,0:T(1,128)}, u32[]{:S(2)}) copy-start(f32[1,256]{1,0:T(1,128)} %get-tuple-element.244) | copy-start | bytes 3076
  255.8 45.1 %copy-start.127 = (f32[32]{0:T(128)S(1)}, f32[32]{0:T(128)}, u32[]{:S(2)}) copy-start(f32[32]{0:T(128)} %get-tuple-element.161) | copy-start | bytes 388
  306.2 48.5 %copy-start.2 = (f32[2,8,196,128]{3,2,1,0:T(8,128)}, f32[2,8,196,128]{3,2,1,0:T(8,128)S(1)}, u32[]{:S(2)}) copy-start(f32[2,8,196,128]{3,2,1,0:T(8,128)S(1)} %get-tuple-element.176) | copy-start | bytes 4816900
  354.7 6.9 copy-start.37
  515.4 128.5 %copy-start.53 = (f32[2,2,1024]{2,1,0:T(2,128)S(1)}, f32[2,2,1024]{2,1,0:T(2,128)}, u32[]{:S(2)}) copy-start(f32[2,2,1024]{2,1,0:T(2,128)} %get-tuple-element.248) | copy-start | bytes 49156
  515.4 128.5 %copy-start.57 = (f32[1024]{0:T(1024)S(1)}, f32[1024]{0:T(1024)}, u32[]{:S(2)}) copy-start(f32[1024]{0:T(1024)} %copy-done.56) | copy-start | bytes 12292
  515.4 215.1 %reduce-scatter.13.cloned.1.call-start = ((), (), s32[]{:S(2)}) async-start(), calls=%async_computation.10 | async-start | bytes 589824
  519.0 279.8 %reduce-scatter.15.cloned.1.call-start = ((), (), s32[]{:S(2)}) async-start(), calls=%async_computation.11 | async-start | bytes 2949120
  657.7 209.1 %reduce-scatter.11.cloned.1.call-start = ((), (), s32[]{:S(2)}) async-start(), calls=%async_computation.9 | async-start | bytes 1327104 | tf_op jit(solution)/shard_map/reduce_scatter | solution.py:328
  664.5 5.6 copy-start.122
  664.5 6.2 copy-start.123
  664.5 6.2 copy-start.124
  664.5 6.7 copy-start.100
  664.5 6.7 copy-start.102
  664.5 7.3 copy-start.27
  677.6 258.8 %reduce-scatter.9.cloned.1.call-start = ((), (), s32[]{:S(2)}) async-start(), calls=%async_computation.8 | async-start | bytes 2211840 | tf_op jit(solution)/shard_map/reduce_scatter | solution.py:325
  697.8 13.0 %copy-start.44 = (bf16[2,1,196,1280]{3,2,1,0:T(8,128)(2,1)S(1)}, bf16[2,1,196,1280]{3,2,1,0:T(8,128)(2,1)}, u32[]{:S(2)}) copy-start(bf16[2,1,196,1280]{3,2,1,0:T(8,128)(2,1)} %copy.211) | copy-start | bytes 3010564
  701.4 9.4 copy-start.11
  701.4 9.4 copy-start.43
  704.0 29.6 %collective-permute-start.5 = (bf16[2,1,196,1280]{3,0,2,1:T(2,128)(2,1)}, bf16[2,1,196,1280]{3,0,2,1:T(2,128)(2,1)}, u32[]{:S(2)}, u32[]{:S(2)}) collective-permute-start(bf16[2,1,196,1280]{3,0,2,1:T(2,128)(2,1)} %copy.239), channel_id=1, source_target_pairs={{1,0},{2,1},{3,2},{4,3},{5,4},{6,5},{7,6},{9,8},{10,9},{11,10},{12... | collective-permute-start | bytes 3010568 | tf_op jit(solution)/shard_map/ppermute | solution.py:24
  705.3 53.4 %collective-permute-start.4 = (bf16[2,1,196,1280]{3,0,2,1:T(2,128)(2,1)S(1)}, bf16[2,1,196,1280]{3,0,2,1:T(2,128)(2,1)}, u32[]{:S(2)}, u32[]{:S(2)}) collective-permute-start(bf16[2,1,196,1280]{3,0,2,1:T(2,128)(2,1)S(1)} %copy.238), channel_id=1, source_target_pairs={{0,1},{1,2},{2,3},{3,4},{4,5},{5,6},{6,7},{8,9},{9,10},{10,11},{11... | collective-permute-start | bytes 3010568 | tf_op jit(solution)/shard_map/ppermute | solution.py:22
  721.2 252.2 %all-reduce.50.cloned.1.call-start = ((), (), s32[]{:S(2)}) async-start(), calls=%async_computation.13 | async-start | bytes 1572864 | tf_op jit(solution)/shard_map/psum | solution.py:319
  770.9 165.7 %copy-start.8 = (f32[2,12,196,128]{3,2,1,0:T(8,128)}, f32[2,12,196,128]{3,2,1,0:T(8,128)S(1)}, u32[]{:S(2)}) copy-start(f32[2,12,196,128]{3,2,1,0:T(8,128)S(1)} %pad_add_fusion.1) | copy-start | bytes 7225348
  936.4 171.5 %all-reduce.46.cloned.1.call-start = ((), (), s32[]{:S(2)}) async-start(), calls=%async_computation.7 | async-start | bytes 1310720 | tf_op jit(solution)/shard_map/psum | solution.py:315
  936.6 8.1 copy-start.15
  936.6 8.1 copy-start.39
  940.7 8.1 collective-permute-start.6
  943.3 7.7 collective-permute-start.7
  953.1 154.8 %copy-start.52 = (f32[9,32,32]{2,1,0:T(8,128)S(1)}, f32[9,32,32]{2,1,0:T(8,128)}, u32[]{:S(2)}) copy-start(f32[9,32,32]{2,1,0:T(8,128)} %get-tuple-element.282) | copy-start | bytes 110596
  953.1 155.5 %copy-start.75 = (f32[32,128]{1,0:T(8,128)S(1)}, f32[32,128]{1,0:T(8,128)}, u32[]{:S(2)}) copy-start(f32[32,128]{1,0:T(8,128)} %get-tuple-element.283) | copy-start | bytes 49156
  (104 other events, 348.7 us)
Sparse Core Ops, SparseCore 0:
  10.3 48.4 all-gather.5
  61.0 47.1 all-gather.3
  110.3 80.7 all-gather.7
  515.5 128.3 all-reduce.47
  647.6 61.6 reduce-scatter.12
  713.1 85.6 reduce-scatter.14
  803.2 63.5 reduce-scatter.10
  870.6 65.7 reduce-scatter.8
  939.5 33.7 all-reduce.49
  979.0 128.8 all-reduce.45
where the time goes:
time: 1130 us; the launch traced here: 1120 us
  waiting for transfers between devices  492 us (44%)
  blocking collectives  278 us (25%)
  local copies, waits for them, and re-layouts  150 us (13%)
  other arithmetic  85.3 us (8%)
  matrix products  70.8 us (6%)
  starting transfers between devices  26 us (2%)
  between operations  17 us (2%)
    psum x4, blocking collectives, norm_forward(): lax.psum((jnp.sum(masked, axis=(0, 1, 2)), jnp.sum(masked * values, axis=...  164 us
    psum x1, waiting for transfers between devices, per_device(): lax.psum((fast_grad_a, fast_grad_b, fast_grad_c, fast_grad_lateral), ('dp...  128 us
    psum x1, waiting for transfers between devices, norm_backward(): lax.psum((jnp.sum(grad_norm_out, axis=(0, 1, 2)), jnp.sum(grad_norm_out *...  125 us
    psum x2, blocking collectives, norm_backward(): lax.psum((jnp.sum(grad_norm_out, axis=(0, 1, 2)), jnp.sum(grad_norm_out *...  81.8 us
    reduce_scatter x1, waiting for transfers between devices, per_device(): lax.psum_scatter(whole[0].astype(jnp.bfloat16), 'mp', scatter_dimension=2...  69.7 us
    reduce_scatter x1, waiting for transfers between devices, per_device(): lax.psum_scatter(whole[1].astype(jnp.bfloat16), 'mp', scatter_dimension=2...  66 us
    ppermute x4, waiting for transfers between devices, padded_2(): lax.ppermute(tail, axis, [(i, (i + 1) % count) for i in range(ends)])  51.1 us
    unnamed x330, local copies, waits for them, and re-layouts  49 us
  transfers between devices with their start and end apart: 18, of which 11 were waited for; matrix products, arithmetic and copies ran while one was open for 18% of the time, Pallas kernels for 0%

commit v1 on v0

--- a/solution.py
+++ b/solution.py
@@ -28,6 +28,39 @@
     return cells
 
 
+def all_sum(parts):
+    sizes = [part.size for part in parts]
+    flat = jnp.concatenate([part.reshape(-1) for part in parts])
+    total = flat.shape[0]
+    flat = jnp.pad(flat, (0, -total % 128))
+    count = lax.axis_size("dp") * lax.axis_size("mp")
+    spread = jnp.broadcast_to(flat[None], (count, flat.shape[0]))
+    flat = jnp.sum(lax.all_to_all(spread, ("dp", "mp"), 0, 0, tiled=True), axis=0)
+    sums = []
+    start = 0
+    for part, size in zip(parts, sizes):
+        sums.append(flat[start : start + size].reshape(part.shape))
+        start += size
+    return sums
+
+
+def all_sum_large(parts):
+    sizes = [part.size for part in parts]
+    flat = jnp.concatenate([part.reshape(-1) for part in parts])
+    total = flat.shape[0]
+    count = lax.axis_size("dp") * lax.axis_size("mp")
+    flat = jnp.pad(flat, (0, -total % (128 * count))).reshape(count, -1)
+    mine = jnp.sum(lax.all_to_all(flat, ("dp", "mp"), 0, 0, tiled=True), axis=0)
+    spread = jnp.broadcast_to(mine[None], flat.shape)
+    flat = lax.all_to_all(spread, ("dp", "mp"), 0, 0, tiled=True).reshape(-1)
+    sums = []
+    start = 0
+    for part, size in zip(parts, sizes):
+        sums.append(flat[start : start + size].reshape(part.shape))
+        start += size
+    return sums
+
+
 def silu_slope(values):
     sigmoid_value = jax.nn.sigmoid(values)
     return sigmoid_value * (1.0 + values * (1.0 - sigmoid_value))
@@ -47,8 +80,8 @@
 
 def norm_forward(values, frame_mask, total_count, affine):
     masked = frame_mask[:, :, None, None] * values
-    totals, squares = lax.psum(
-        (jnp.sum(masked, axis=(0, 1, 2)), jnp.sum(masked * values, axis=(0, 1, 2))), ("dp", "mp")
+    totals, squares = all_sum(
+        (jnp.sum(masked, axis=(0, 1, 2)), jnp.sum(masked * values, axis=(0, 1, 2)))
     )
     average = totals / total_count
     inverse_std = lax.rsqrt(squares / total_count - average * average + NORM_EPSILON)
@@ -57,9 +90,8 @@
 
 
 def norm_backward(grad_norm_out, standard, inverse_std, frame_mask, total_count, affine):
-    grad_beta, grad_gamma = lax.psum(
-        (jnp.sum(grad_norm_out, axis=(0, 1, 2)), jnp.sum(grad_norm_out * standard, axis=(0, 1, 2))),
-        ("dp", "mp"),
+    grad_beta, grad_gamma = all_sum(
+        (jnp.sum(grad_norm_out, axis=(0, 1, 2)), jnp.sum(grad_norm_out * standard, axis=(0, 1, 2)))
     )
     grad_values = (
         frame_mask[:, :, None, None]
@@ -312,8 +344,8 @@
     grad_fast_in = (fast_keep * (d_padded_fast[:, 2:-2] + fast_edges + fast_cot)).astype(
         jnp.bfloat16
     )
-    summed_a, summed_b, summed_c, summed_lateral = lax.psum(
-        (fast_grad_a, fast_grad_b, fast_grad_c, fast_grad_lateral), ("dp", "mp")
+    summed_a, summed_b, summed_c, summed_lateral = all_sum_large(
+        (fast_grad_a, fast_grad_b, fast_grad_c, fast_grad_lateral)
     )
     whole = (
         lax.psum(slow_grad_a.astype(jnp.bfloat16), "dp").astype(jnp.float32),

time: 1130 us -> 699 us (0.62)
  waiting for transfers between devices: 492 us -> 234 us
  blocking collectives: 278 us -> 33.2 us
  starting transfers between devices: 26 us -> 88.5 us
  local copies, waits for them, and re-layouts: 150 us -> 167 us
    psum x2 -> x0, waiting for transfers between devices: 253 us -> none  [the longest x1 128 us: per_device(): lax.psum((fast_grad_a, fast_grad_b, fast_grad_c, fast_grad_lateral), ('dp...]
    psum x6 -> x0, blocking collectives: 246 us -> none  [the longest x4 164 us: norm_forward(): lax.psum((jnp.sum(masked, axis=(0, 1, 2)), jnp.sum(masked * values, axis=...]
    all_to_all x0 -> x16, waiting for transfers between devices: none -> 103 us  [the longest x14 87.2 us: all_sum(): lax.all_to_all(spread, ('dp', 'mp'), 0, 0, tiled=True)]
    all_to_all x0 -> x16, starting transfers between devices: none -> 62 us  [the longest x14 55.3 us: all_sum(): lax.all_to_all(spread, ('dp', 'mp'), 0, 0, tiled=True)]
    reduce_scatter x1, waiting for transfers between devices: 66 us -> 7.69 us  [per_device(): lax.psum_scatter(whole[1].astype(jnp.bfloat16), 'mp', scatter_dimension=2...]
    ppermute x4, waiting for transfers between devices: 51.1 us -> 20.2 us  [padded_2(): lax.ppermute(tail, axis, [(i, (i + 1) % count) for i in range(ends)])]
    unnamed x12 -> x10, waiting for transfers between devices: 29.4 us -> 1.48 us
    unnamed x330 -> x304, local copies, waits for them, and re-layouts: 49 us -> 39.7 us
  transfers between devices with their start and end apart: 18 -> 32, of which waited for: 11 -> 17; matrix products, arithmetic and copies ran while one was open for 18% -> 40% of each run, Pallas kernels for 0% -> 0%
where the time goes in v1:
time: 699 us; the launch traced here: 687 us
  waiting for transfers between devices  234 us (33%)
  local copies, waits for them, and re-layouts  167 us (24%)
  starting transfers between devices  88.5 us (13%)
  other arithmetic  80.5 us (12%)
  matrix products  67.5 us (10%)
  blocking collectives  33.2 us (5%)
  between operations  17.4 us (2%)
    all_to_all x14, waiting for transfers between devices, all_sum(): lax.all_to_all(spread, ('dp', 'mp'), 0, 0, tiled=True)  87.2 us
    reduce_scatter x1, waiting for transfers between devices, per_device(): lax.psum_scatter(whole[0].astype(jnp.bfloat16), 'mp', scatter_dimension=2...  71.2 us
    all_to_all x14, starting transfers between devices, all_sum(): lax.all_to_all(spread, ('dp', 'mp'), 0, 0, tiled=True)  55.3 us
    unnamed x304, local copies, waits for them, and re-layouts  39.7 us
    all_gather x1, blocking collectives, per_device(): lax.all_gather(w_slow_c, 'mp', axis=1, tiled=True)  33.2 us
    concatenate x18, local copies, waits for them, and re-layouts, spatial_patches(): jnp.concatenate(pieces, -1)  30.1 us
    dot_general x8, matrix products, back_product(): jnp.einsum('abpd,cd->abpc', upstream, weights, preferred_element_type=jnp...  24.8 us
    dot_general x8, matrix products, outer_sum(): jnp.einsum('abpc,abpd->cd', left_side, right_side, preferred_element_type...  23.6 us
  transfers between devices with their start and end apart: 32, of which 17 were waited for; matrix products, arithmetic and copies ran while one was open for 40% of the time, Pallas kernels for 0%

profile of v1, /device:TPU:0, one launch (start us, length us, event | category | flops | bytes accessed | tf_op | source)
XLA Modules:
  0.0 687.3 jit_solution(12090155958844667161)
XLA Ops:
  12.0 5.6 collective-permute-start
  23.7 33.2 %all_gather.14 = bf16[256,1024]{1,0:T(8,128)(2,1)} all-gather(bf16[256,128]{1,0:T(8,128)(2,1)S(1)} %copy-done.59), channel_id=1, replica_groups=mesh['dp'=4,'mp'=8] {'mp'}, dimensions={1}, use_global_device_ids=true | all-gather | bytes 589824 | tf_op jit(solution)/shard_map/all_gather | solution.py:240
  65.7 3.1 all-to-all-start
  78.8 5.1 pad_slice_fusion
  103.6 6.0 all-to-all-start.1
  116.3 5.6 collective-permute-start.2
  124.8 4.9 all-to-all-start.2
  130.4 36.0 %all-to-all-done.2 = f32[32,1,256]{2,1,0:T(1,128)S(1)} async-done(((f32[32,1,256]{2,1,0:T(1,128)}), f32[32,1,256]{2,1,0:T(1,128)S(1)}, u32[]{:S(2)}, u32[]{:S(2)}) %all-to-all-start.2) | async-done | bytes 32800 | tf_op jit(solution)/shard_map/all_to_all | solution.py:38
  166.6 3.4 fusion.75
  170.7 5.8 all-to-all-start.11
  182.3 4.0 copy.366
  186.2 4.5 multiply_reduce_fusion.7
  191.5 6.2 all-to-all-start.3
  200.2 4.7 all-to-all-done.3
  238.0 7.3 %all-to-all-done.4 = f32[32,1,512]{2,1,0:T(1,128)S(1)} async-done(((f32[32,1,512]{2,1,0:T(1,128)}), f32[32,1,512]{2,1,0:T(1,128)S(1)}, u32[]{:S(2)}, u32[]{:S(2)}) %all-to-all-start.4) | async-done | bytes 65568 | tf_op jit(solution)/shard_map/all_to_all | solution.py:38
  246.0 4.7 fusion.11
  250.7 2.9 multiply_reduce_fusion.1
  254.5 3.3 all-to-all-start.6
  260.7 7.7 %all-to-all-done.6 = f32[32,1,2048]{2,1,0:T(1,128)} async-done(((f32[32,1,2048]{2,1,0:T(1,128)}), f32[32,1,2048]{2,1,0:T(1,128)}, u32[]{:S(2)}, u32[]{:S(2)}) %all-to-all-start.6) | async-done | bytes 262176 | tf_op jit(solution)/shard_map/all_to_all | solution.py:38
  269.3 2.6 all-to-all-start.5
  275.3 7.2 %all-to-all-done.5 = f32[32,1,2048]{2,1,0:T(1,128)S(1)} async-done(((f32[32,1,2048]{2,1,0:T(1,128)}), f32[32,1,2048]{2,1,0:T(1,128)S(1)}, u32[]{:S(2)}, u32[]{:S(2)}) %all-to-all-start.5) | async-done | bytes 262176 | tf_op jit(solution)/shard_map/all_to_all | solution.py:38
  283.1 2.7 all-to-all-start.12
  286.1 6.7 multiply_reduce_fusion.2
  293.7 5.9 all-to-all-start.10
  301.9 8.4 %all-to-all-done.10 = f32[32,1,2048]{2,1,0:T(1,128)} async-done(((f32[32,1,2048]{2,1,0:T(1,128)}), f32[32,1,2048]{2,1,0:T(1,128)}, u32[]{:S(2)}, u32[]{:S(2)}) %all-to-all-start.10) | async-done | bytes 262176 | tf_op jit(solution)/shard_map/all_to_all | solution.py:38
  311.1 2.6 all-to-all-start.7
  313.8 7.1 %fusion.46 = f32[16,14,14,9,32]{4,0,3,2,1:T(8,128)} fusion(bf16[16,14,14,32,1]{3,0,4,2,1:T(8,128)(2,1)S(1)} %bitcast.332, bf16[9,32,32]{2,1,0:T(8,128)(2,1)S(1)} %copy-done.51), kind=kOutput, calls=%fused_computation.203 | convolution fusion | flops 57802752 | bytes 3831808 | tf_op jit(solution)/shard_map/abpd,cd->abpc/dot_general | solution.py:78
  324.6 5.8 multiply_convert_fusion
  333.7 10.1 %slice_bitcast_fusion.8 = (f32[16,14,14,32]{3,0,2,1:T(8,128)}, f32[16,14,14,32]{3,0,2,1:T(8,128)S(1)}, f32[16,14,14,32]{3,0,2,1:T(8,128)}, f32[16,14,14,32]{3,0,...) fusion(f32[16,14,14,9,32]{4,0,3,2,1:T(8,128)} %fusion.46), kind=kLoop, calls=%fused_computation.76 | loop fusion | bytes 7225344 | tf_op jit(solution)/shard_map/squeeze | solution.py:125
  343.8 4.3 pad_add_fusion.2
  348.0 4.2 bitcast_convert_fusion
  352.2 4.5 copy.458
  356.7 5.6 pad_add_fusion.4
  362.4 2.9 copy.415
  367.7 3.6 all-to-all-start.13
  371.3 3.1 convolution_bitcast_fusion.4
  375.4 2.9 all-to-all-done.13
  381.3 3.5 fusion.48
  384.8 6.5 copy.421
  391.3 2.9 fusion.77
  394.9 3.3 all-to-all-start.8
  398.3 7.2 %all-to-all-done.8 = f32[32,1,512]{2,1,0:T(1,128)S(1)} async-done(((f32[32,1,512]{2,1,0:T(1,128)}), f32[32,1,512]{2,1,0:T(1,128)S(1)}, u32[]{:S(2)}, u32[]{:S(2)}) %all-to-all-start.8) | async-done | bytes 65568 | tf_op jit(solution)/shard_map/all_to_all | solution.py:38
  413.9 2.6 all-to-all-start.9
  416.5 4.9 bitcast_convert_fusion.1
  421.4 3.4 all-to-all-done.9
  426.3 6.3 fusion.95
  432.6 8.9 %fusion.82 = (f32[2,2,196,1280]{3,2,1,0:T(8,128)S(1)}, f32[2,2,196,1280]{3,2,1,0:T(8,128)}, f32[2,2,196,1280]{3,2,1,0:T(8,128)}) fusion(f32[2,2,196,3840]{3,2,1,0:T(8,128)} %fusion.95), kind=kLoop, calls=%fused_computation.314 | loop fusion | bytes 24084480 | tf_op jit(solution)/shard_map/slice | solution.py:139
  441.5 3.6 fusion.16
  448.9 5.7 collective-permute-start.4
  454.6 5.7 fusion.2
  460.3 4.0 copy.420
  464.3 5.0 pad_add_fusion
  469.4 7.1 %collective-permute-done.5 = bf16[2,1,196,1280]{3,0,2,1:T(2,128)(2,1)} collective-permute-done((bf16[2,1,196,1280]{3,0,2,1:T(2,128)(2,1)}, bf16[2,1,196,1280]{3,0,2,1:T(2,128)(2,1)}, u32[]{:S(2)}, u32[]{:S(2)}) %collective-permute-start.5) | collective-permute-done | bytes 1003552 | tf_op jit(solution)/shard_map/ppermute | solution.py:24
  477.9 20.2 %collective-permute-done.4 = bf16[2,1,196,1280]{3,0,2,1:T(2,128)(2,1)} collective-permute-done((bf16[2,1,196,1280]{3,0,2,1:T(2,128)(2,1)S(1)}, bf16[2,1,196,1280]{3,0,2,1:T(2,128)(2,1)}, u32[]{:S(2)}, u32[]{:S(2)}) %collective-permute-start.4) | collective-permute-done | bytes 1003552 | tf_op jit(solution)/shard_map/ppermute | solution.py:22
  506.3 4.1 all-to-all-start.14
  511.1 2.8 fusion.83
  515.3 2.8 copy.424
  521.0 15.4 %all-to-all-done.14 = f32[32,1,6016]{2,1,0:T(1,128)S(1)} async-done(((f32[32,1,6016]{2,1,0:T(1,128)}), f32[32,1,6016]{2,1,0:T(1,128)S(1)}, u32[]{:S(2)}, u32[]{:S(2)}) %all-to-all-start.14) | async-done | bytes 770080 | tf_op jit(solution)/shard_map/all_to_all | solution.py:53
  538.1 2.6 all-to-all-start.15
  544.7 3.7 collective-permute-start.6
  552.8 2.8 copy.426
  557.6 7.7 %reduce-scatter.11.cloned.1.call-done = bf16[9,256,32]{1,2,0:T(8,128)(2,1)} async-done(((bf16[9,256,256]{1,2,0:T(8,128)(2,1)}), bf16[9,256,32]{1,2,0:T(8,128)(2,1)}) %reduce-scatter.11.cloned.1.call-update) | async-done | bytes 147472 | tf_op jit(solution)/shard_map/reduce_scatter | solution.py:360
  565.3 71.2 %reduce-scatter.9.cloned.1.call-done = bf16[3,1280,32]{1,2,0:T(8,128)(2,1)} async-done(((bf16[3,1280,256]{1,2,0:T(8,128)(2,1)}), bf16[3,1280,32]{1,2,0:T(8,128)(2,1)}) %reduce-scatter.9.cloned.1.call-update) | async-done | bytes 245776 | tf_op jit(solution)/shard_map/reduce_scatter | solution.py:357
  650.2 23.3 %all-reduce.42.cloned.1.call-done = (bf16[3,1280,32]{1,2,0:T(8,128)(2,1)}, bf16[9,256,32]{1,2,0:T(8,128)(2,1)}, bf16[256,128]{1,0:T(8,128)(2,1)}, bf16[1280,128]{1,0:T(8,128)(2,1)}) async-done(((bf16[3,1280,32]{1,2,0:T(8,128)(2,1)}, bf16[9,256,32]{1,2,0:T(8,128)(2,1)}, bf16[256,128]{1,0:T(8,128)(2,1)}, bf16[1280,128]{1,0:T(8,128)(2,1)}), (bf16[3,1280,32]{1,2,0:T(8,128)(2,1)}, bf16[9,256,32]{1,2,0:T(8,128)(2,1)}, ...) | async-done | bytes 786448 | tf_op jit(solution)/shard_map/psum | solution.py:351
  (519 shorter events, 188.7 us)
Async XLA Ops:
  7.2 65.6 %copy-start = (bf16[5,128,256]{2,1,0:T(8,128)(2,1)S(1)}, bf16[5,128,256]{2,1,0:T(8,128)(2,1)}, u32[]{:S(2)}) copy-start(bf16[5,128,256]{2,1,0:T(8,128)(2,1)} %param.26) | copy-start | bytes 983044
  7.3 15.2 %copy-start.101 = (f32[2,1024]{1,0:T(2,128)S(1)}, f32[2,1024]{1,0:T(2,128)}, u32[]{:S(2)}) copy-start(f32[2,1024]{1,0:T(2,128)} %param.36) | copy-start | bytes 24580
  7.3 15.8 %copy-start.102 = (f32[2,1024]{1,0:T(2,128)S(1)}, f32[2,1024]{1,0:T(2,128)}, u32[]{:S(2)}) copy-start(f32[2,1024]{1,0:T(2,128)} %param.37) | copy-start | bytes 24580
  7.3 16.4 %copy-start.77 = (bf16[3,128,32]{1,2,0:T(8,128)(2,1)S(1)}, bf16[3,128,32]{1,2,0:T(8,128)(2,1)}, u32[]{:S(2)}) copy-start(bf16[3,128,32]{1,2,0:T(8,128)(2,1)} %param.23) | copy-start | bytes 73732
  7.3 16.4 %copy-start.59 = (bf16[256,128]{1,0:T(8,128)(2,1)S(1)}, bf16[256,128]{1,0:T(8,128)(2,1)}, u32[]{:S(2)}) copy-start(bf16[256,128]{1,0:T(8,128)(2,1)} %param.29) | copy-start | bytes 196612
  7.3 175.0 %all-gather.4.cloned.1.call-start = ((), (), s32[]{:S(2)}) async-start(), calls=%async_computation.20 | async-start | bytes 2211840 | tf_op jit(solution)/shard_map/all_gather | solution.py:238
  8.0 189.8 %all-gather.6.cloned.1.call-start = ((), (), s32[]{:S(2)}) async-start(), calls=%async_computation.21 | async-start | bytes 1327104 | tf_op jit(solution)/shard_map/all_gather | solution.py:239
  8.8 237.1 %all-gather.8.cloned.1.call-start = ((), (), s32[]{:S(2)}) async-start(), calls=%async_computation.22 | async-start | bytes 2949120 | tf_op jit(solution)/shard_map/all_gather | solution.py:241
  10.2 66.7 %copy-start.52 = (f32[2,8]{1,0:T(2,128)}, f32[2,8]{1,0:T(2,128)S(1)}, u32[]{:S(2)}) copy-start(f32[2,8]{1,0:T(2,128)S(1)} %get-tuple-element.285) | copy-start | bytes 196
  12.0 58.8 %copy-start.14 = (bf16[2,8,196,128]{3,2,1,0:T(8,128)(2,1)}, bf16[2,8,196,128]{3,2,1,0:T(8,128)(2,1)S(1)}, u32[]{:S(2)}) copy-start(bf16[2,8,196,128]{3,2,1,0:T(8,128)(2,1)S(1)} %copy_multiply_fusion) | copy-start | bytes 2408452
  12.0 49.3 %collective-permute-start = (bf16[2,2,196,128]{3,2,1,0:T(8,128)(2,1)S(1)}, bf16[2,2,196,128]{3,2,1,0:T(8,128)(2,1)}, u32[]{:S(2)}, u32[]{:S(2)}) collective-permute-start(bf16[2,2,196,128]{3,2,1,0:T(8,128)(2,1)S(1)} %get-tuple-element.224), channel_id=1, source_target_pairs={{0,1},{1,2},{2,3},{3,4},{4,5},{5,6},{6,7},{8,9},{9,10},{10,11},{11... | collective-permute-start | bytes 602120 | tf_op jit(solution)/shard_map/ppermute | solution.py:22
  17.6 44.7 %collective-permute-start.1 = (bf16[2,2,196,128]{3,2,1,0:T(8,128)(2,1)S(1)}, bf16[2,2,196,128]{3,2,1,0:T(8,128)(2,1)S(1)}, u32[]{:S(2)}, u32[]{:S(2)}) collective-permute-start(bf16[2,2,196,128]{3,2,1,0:T(8,128)(2,1)S(1)} %get-tuple-element.225), channel_id=1, source_target_pairs={{1,0},{2,1},{3,2},{4,3},{5,4},{6,5},{7,6},{9,8},{10,9},{11,10},{12... | collective-permute-start | bytes 602120 | tf_op jit(solution)/shard_map/ppermute | solution.py:24
  20.8 56.2 %copy-start.95 = (f32[32]{0:T(128)}, f32[32]{0:T(128)S(1)}, u32[]{:S(2)}) copy-start(f32[32]{0:T(128)S(1)} %get-tuple-element.282) | copy-start | bytes 388
  20.8 56.2 %copy-start.98 = (f32[32]{0:T(128)}, f32[32]{0:T(128)S(1)}, u32[]{:S(2)}) copy-start(f32[32]{0:T(128)S(1)} %get-tuple-element.283) | copy-start | bytes 388
  23.1 35.7 %copy-start.131 = (s32[2]{0:T(128)S(1)}, s32[2]{0:T(128)}, u32[]{:S(2)}) copy-start(s32[2]{0:T(128)} %iota_add_fusion) | copy-start | bytes 28
  23.7 39.8 %copy-start.56 = (bf16[384,32,1,1]{0,1,2,3:T(8,128)(2,1)}, bf16[384,32,1,1]{0,1,2,3:T(8,128)(2,1)S(1)}, u32[]{:S(2)}) copy-start(bf16[384,32,1,1]{0,1,2,3:T(8,128)(2,1)S(1)} %reshape.429) | copy-start | bytes 73732
  65.7 10.6 %all-to-all-start = ((f32[32,1,128]{2,1,0:T(1,128)}), f32[32,1,128]{2,1,0:T(1,128)S(1)}, u32[]{:S(2)}, u32[]{:S(2)}) async-start(f32[32,1,128]{2,1,0:T(1,128)} %broadcast_in_dim.44), calls=%async_computation | async-start | bytes 32768 | tf_op jit(solution)/shard_map/all_to_all | solution.py:38
  76.9 23.4 %copy-start.78 = (f32[32]{0:T(128)}, f32[32]{0:T(128)S(1)}, u32[]{:S(2)}) copy-start(f32[32]{0:T(128)S(1)} %get-tuple-element.167) | copy-start | bytes 388
  76.9 23.4 %copy-start.80 = (f32[32]{0:T(128)}, f32[32]{0:T(128)S(1)}, u32[]{:S(2)}) copy-start(f32[32]{0:T(128)S(1)} %get-tuple-element.168) | copy-start | bytes 388
  102.8 19.1 %copy-start.20 = (f32[2,8,196,32]{2,3,1,0:T(8,128)}, f32[2,8,196,32]{2,3,1,0:T(8,128)S(1)}, u32[]{:S(2)}) copy-start(f32[2,8,196,32]{2,3,1,0:T(8,128)S(1)} %get-tuple-element.301) | copy-start | bytes 1204228
  103.6 18.3 %all-to-all-start.1 = ((f32[32,1,128]{2,1,0:T(1,128)}), f32[32,1,128]{2,1,0:T(1,128)S(1)}, u32[]{:S(2)}, u32[]{:S(2)}) async-start(f32[32,1,128]{2,1,0:T(1,128)} %broadcast_in_dim.45), calls=%async_computation.1 | async-start | bytes 32768 | tf_op jit(solution)/shard_map/all_to_all | solution.py:38
  114.8 14.9 %copy-start.120 = (f32[32]{0:T(128)S(1)}, f32[32]{0:T(128)}, u32[]{:S(2)}) copy-start(f32[32]{0:T(128)} %get-tuple-element.166) | copy-start | bytes 388
  114.8 51.7 %copy-start.116 = (f32[2,128]{1,0:T(2,128)S(1)}, f32[2,128]{1,0:T(2,128)}, u32[]{:S(2)}) copy-start(f32[2,128]{1,0:T(2,128)} %param.33) | copy-start | bytes 3076
  114.8 51.7 %copy-start.54 = (f32[2,8]{1,0:T(2,128)S(1)}, f32[2,8]{1,0:T(2,128)}, u32[]{:S(2)}) copy-start(f32[2,8]{1,0:T(2,128)} %copy-done.52) | copy-start | bytes 196
  114.8 51.7 %copy-start.104 = (bf16[2,8]{1,0:T(2,128)(2,1)S(1)}, bf16[2,8]{1,0:T(2,128)(2,1)}, u32[]{:S(2)}) copy-start(bf16[2,8]{1,0:T(2,128)(2,1)} %copy-done.103) | copy-start | bytes 100
  114.9 51.7 %copy-start.118 = (f32[128]{0:T(128)S(1)}, f32[128]{0:T(128)}, u32[]{:S(2)}) copy-start(f32[128]{0:T(128)} %get-tuple-element.278) | copy-start | bytes 1540
  114.9 51.7 %copy-start.119 = (f32[128]{0:T(128)S(1)}, f32[128]{0:T(128)}, u32[]{:S(2)}) copy-start(f32[128]{0:T(128)} %get-tuple-element.279) | copy-start | bytes 1540
  114.9 62.6 %collective-permute-start.3 = (bf16[2,1,196,1280]{3,0,2,1:T(2,128)(2,1)}, bf16[2,1,196,1280]{3,0,2,1:T(2,128)(2,1)}, u32[]{:S(2)}, u32[]{:S(2)}) collective-permute-start(bf16[2,1,196,1280]{3,0,2,1:T(2,128)(2,1)} %copy.364), channel_id=1, source_target_pairs={{1,0},{2,1},{3,2},{4,3},{5,4},{6,5},{7,6},{9,8},{10,9},{11,10},{12... | collective-permute-start | bytes 3010568 | tf_op jit(solution)/shard_map/ppermute | solution.py:24
  116.3 63.6 %collective-permute-start.2 = (bf16[2,1,196,1280]{3,0,2,1:T(2,128)(2,1)}, bf16[2,1,196,1280]{3,0,2,1:T(2,128)(2,1)}, u32[]{:S(2)}, u32[]{:S(2)}) collective-permute-start(bf16[2,1,196,1280]{3,0,2,1:T(2,128)(2,1)} %copy.362), channel_id=1, source_target_pairs={{0,1},{1,2},{2,3},{3,4},{4,5},{5,6},{6,7},{8,9},{9,10},{10,11},{11... | collective-permute-start | bytes 3010568 | tf_op jit(solution)/shard_map/ppermute | solution.py:22
  124.8 41.7 %all-to-all-start.2 = ((f32[32,1,256]{2,1,0:T(1,128)}), f32[32,1,256]{2,1,0:T(1,128)S(1)}, u32[]{:S(2)}, u32[]{:S(2)}) async-start(f32[32,1,256]{2,1,0:T(1,128)} %broadcast_in_dim.46), calls=%async_computation.2 | async-start | bytes 65536 | tf_op jit(solution)/shard_map/all_to_all | solution.py:38
  169.9 87.9 %copy-start.2 = (f32[2,8,196,128]{3,2,1,0:T(8,128)}, f32[2,8,196,128]{3,2,1,0:T(8,128)S(1)}, u32[]{:S(2)}) copy-start(f32[2,8,196,128]{3,2,1,0:T(8,128)S(1)} %get-tuple-element.176) | copy-start | bytes 4816900
  170.7 20.1 %all-to-all-start.11 = ((f32[32,1,256]{2,1,0:T(1,128)}), f32[32,1,256]{2,1,0:T(1,128)S(1)}, u32[]{:S(2)}, u32[]{:S(2)}) async-start(f32[32,1,256]{2,1,0:T(1,128)} %broadcast_in_dim.55), calls=%async_computation.11 | async-start | bytes 65536 | tf_op jit(solution)/shard_map/all_to_all | solution.py:38
  190.8 14.8 %copy-start.85 = (f32[1,256]{1,0:T(1,128)S(1)}, f32[1,256]{1,0:T(1,128)}, u32[]{:S(2)}) copy-start(f32[1,256]{1,0:T(1,128)} %get-tuple-element.265) | copy-start | bytes 3076
  191.5 13.5 %all-to-all-start.3 = ((f32[32,1,512]{2,1,0:T(1,128)}), f32[32,1,512]{2,1,0:T(1,128)S(1)}, u32[]{:S(2)}, u32[]{:S(2)}) async-start(f32[32,1,512]{2,1,0:T(1,128)} %broadcast_in_dim.47), calls=%async_computation.3 | async-start | bytes 131072 | tf_op jit(solution)/shard_map/all_to_all | solution.py:38
  205.6 25.8 %copy-start.71 = (f32[256]{0:T(256)}, f32[256]{0:T(256)S(1)}, u32[]{:S(2)}) copy-start(f32[256]{0:T(256)S(1)} %get-tuple-element.178) | copy-start | bytes 3076
  205.6 25.8 %copy-start.73 = (f32[256]{0:T(256)}, f32[256]{0:T(256)S(1)}, u32[]{:S(2)}) copy-start(f32[256]{0:T(256)S(1)} %get-tuple-element.179) | copy-start | bytes 3076
  235.4 9.9 %all-to-all-start.4 = ((f32[32,1,512]{2,1,0:T(1,128)}), f32[32,1,512]{2,1,0:T(1,128)S(1)}, u32[]{:S(2)}, u32[]{:S(2)}) async-start(f32[32,1,512]{2,1,0:T(1,128)} %broadcast_in_dim.48), calls=%async_computation.4 | async-start | bytes 131072 | tf_op jit(solution)/shard_map/all_to_all | solution.py:38
  245.9 84.4 %copy-start.105 = (f32[256]{0:T(256)}, f32[256]{0:T(256)S(1)}, u32[]{:S(2)}) copy-start(f32[256]{0:T(256)S(1)} %get-tuple-element.182) | copy-start | bytes 3076
  245.9 84.4 %copy-start.107 = (f32[256]{0:T(256)}, f32[256]{0:T(256)S(1)}, u32[]{:S(2)}) copy-start(f32[256]{0:T(256)S(1)} %get-tuple-element.183) | copy-start | bytes 3076
  254.5 13.9 %all-to-all-start.6 = ((f32[32,1,2048]{2,1,0:T(1,128)}), f32[32,1,2048]{2,1,0:T(1,128)}, u32[]{:S(2)}, u32[]{:S(2)}) async-start(f32[32,1,2048]{2,1,0:T(1,128)} %broadcast_in_dim.50), calls=%async_computation.6 | async-start | bytes 524288 | tf_op jit(solution)/shard_map/all_to_all | solution.py:38
  260.7 25.3 %copy-start.69 = (f32[1,1024]{1,0:T(1,128)S(1)}, f32[1,1024]{1,0:T(1,128)}, u32[]{:S(2)}) copy-start(f32[1,1024]{1,0:T(1,128)} %get-tuple-element.252) | copy-start | bytes 12292
  260.7 25.4 %copy-start.83 = (f32[1,1024]{1,0:T(1,128)S(1)}, f32[1,1024]{1,0:T(1,128)}, u32[]{:S(2)}) copy-start(f32[1,1024]{1,0:T(1,128)} %get-tuple-element.253) | copy-start | bytes 12292
  260.7 25.4 %copy-start.84 = (f32[1,1024]{1,0:T(1,128)S(1)}, f32[1,1024]{1,0:T(1,128)}, u32[]{:S(2)}) copy-start(f32[1,1024]{1,0:T(1,128)} %get-tuple-element.255) | copy-start | bytes 12292
  269.3 13.2 %all-to-all-start.5 = ((f32[32,1,2048]{2,1,0:T(1,128)}), f32[32,1,2048]{2,1,0:T(1,128)S(1)}, u32[]{:S(2)}, u32[]{:S(2)}) async-start(f32[32,1,2048]{2,1,0:T(1,128)} %broadcast_in_dim.49), calls=%async_computation.5 | async-start | bytes 524288 | tf_op jit(solution)/shard_map/all_to_all | solution.py:38
  283.1 9.8 %all-to-all-start.12 = ((f32[32,1,128]{2,1,0:T(1,128)}), f32[32,1,128]{2,1,0:T(1,128)S(1)}, u32[]{:S(2)}, u32[]{:S(2)}) async-start(f32[32,1,128]{2,1,0:T(1,128)} %broadcast_in_dim.56), calls=%async_computation.12 | async-start | bytes 32768 | tf_op jit(solution)/shard_map/all_to_all | solution.py:38
  292.7 21.0 %copy-start.51 = (bf16[9,32,32]{2,1,0:T(8,128)(2,1)S(1)}, bf16[9,32,32]{2,1,0:T(8,128)(2,1)}, u32[]{:S(2)}) copy-start(bf16[9,32,32]{2,1,0:T(8,128)(2,1)} %param.24) | copy-start | bytes 55300
  293.7 16.5 %all-to-all-start.10 = ((f32[32,1,2048]{2,1,0:T(1,128)}), f32[32,1,2048]{2,1,0:T(1,128)}, u32[]{:S(2)}, u32[]{:S(2)}) async-start(f32[32,1,2048]{2,1,0:T(1,128)} %broadcast_in_dim.54), calls=%async_computation.10 | async-start | bytes 524288 | tf_op jit(solution)/shard_map/all_to_all | solution.py:38
  301.1 19.8 %copy-start.18 = (bf16[2,8,196,32]{2,3,1,0:T(8,128)(2,1)}, bf16[2,8,196,32]{2,3,1,0:T(8,128)(2,1)S(1)}, u32[]{:S(2)}) copy-start(bf16[2,8,196,32]{2,3,1,0:T(8,128)(2,1)S(1)} %multiply_convert_fusion.10) | copy-start | bytes 602116
  311.1 13.2 %all-to-all-start.7 = ((f32[32,1,2048]{2,1,0:T(1,128)}), f32[32,1,2048]{2,1,0:T(1,128)S(1)}, u32[]{:S(2)}, u32[]{:S(2)}) async-start(f32[32,1,2048]{2,1,0:T(1,128)} %broadcast_in_dim.51), calls=%async_computation.7 | async-start | bytes 524288 | tf_op jit(solution)/shard_map/all_to_all | solution.py:38
  313.7 237.5 %reduce-scatter.13.cloned.1.call-start = ((), (), s32[]{:S(2)}) async-start(), calls=%async_computation.25 | async-start | bytes 589824
  333.4 222.2 %reduce-scatter.15.cloned.1.call-start = ((), (), s32[]{:S(2)}) async-start(), calls=%async_computation.26 | async-start | bytes 2949120
  367.7 10.7 %all-to-all-start.13 = ((f32[32,1,128]{2,1,0:T(1,128)}), f32[32,1,128]{2,1,0:T(1,128)S(1)}, u32[]{:S(2)}, u32[]{:S(2)}) async-start(f32[32,1,128]{2,1,0:T(1,128)} %broadcast_in_dim.57), calls=%async_computation.13 | async-start | bytes 32768 | tf_op jit(solution)/shard_map/all_to_all | solution.py:38
  394.9 10.6 %all-to-all-start.8 = ((f32[32,1,512]{2,1,0:T(1,128)}), f32[32,1,512]{2,1,0:T(1,128)S(1)}, u32[]{:S(2)}, u32[]{:S(2)}) async-start(f32[32,1,512]{2,1,0:T(1,128)} %broadcast_in_dim.52), calls=%async_computation.8 | async-start | bytes 131072 | tf_op jit(solution)/shard_map/all_to_all | solution.py:38
  413.9 11.0 %all-to-all-start.9 = ((f32[32,1,512]{2,1,0:T(1,128)}), f32[32,1,512]{2,1,0:T(1,128)S(1)}, u32[]{:S(2)}, u32[]{:S(2)}) async-start(f32[32,1,512]{2,1,0:T(1,128)} %broadcast_in_dim.53), calls=%async_computation.9 | async-start | bytes 131072 | tf_op jit(solution)/shard_map/all_to_all | solution.py:38
  416.4 148.8 %reduce-scatter.11.cloned.1.call-start = ((), (), s32[]{:S(2)}) async-start(), calls=%async_computation.24 | async-start | bytes 1327104 | tf_op jit(solution)/shard_map/reduce_scatter | solution.py:360
  421.4 215.0 %reduce-scatter.9.cloned.1.call-start = ((), (), s32[]{:S(2)}) async-start(), calls=%async_computation.23 | async-start | bytes 2211840 | tf_op jit(solution)/shard_map/reduce_scatter | solution.py:357
  447.6 28.9 %collective-permute-start.5 = (bf16[2,1,196,1280]{3,0,2,1:T(2,128)(2,1)}, bf16[2,1,196,1280]{3,0,2,1:T(2,128)(2,1)}, u32[]{:S(2)}, u32[]{:S(2)}) collective-permute-start(bf16[2,1,196,1280]{3,0,2,1:T(2,128)(2,1)} %copy.398), channel_id=1, source_target_pairs={{1,0},{2,1},{3,2},{4,3},{5,4},{6,5},{7,6},{9,8},{10,9},{11,10},{12... | collective-permute-start | bytes 3010568 | tf_op jit(solution)/shard_map/ppermute | solution.py:24
  448.9 49.2 %collective-permute-start.4 = (bf16[2,1,196,1280]{3,0,2,1:T(2,128)(2,1)S(1)}, bf16[2,1,196,1280]{3,0,2,1:T(2,128)(2,1)}, u32[]{:S(2)}, u32[]{:S(2)}) collective-permute-start(bf16[2,1,196,1280]{3,0,2,1:T(2,128)(2,1)S(1)} %copy.397), channel_id=1, source_target_pairs={{0,1},{1,2},{2,3},{3,4},{4,5},{5,6},{6,7},{8,9},{9,10},{10,11},{11... | collective-permute-start | bytes 3010568 | tf_op jit(solution)/shard_map/ppermute | solution.py:22
  506.3 30.1 %all-to-all-start.14 = ((f32[32,1,6016]{2,1,0:T(1,128)}), f32[32,1,6016]{2,1,0:T(1,128)S(1)}, u32[]{:S(2)}, u32[]{:S(2)}) async-start(f32[32,1,6016]{2,1,0:T(1,128)} %bitcast.93), calls=%async_computation.14 | async-start | bytes 1540096 | tf_op jit(solution)/shard_map/all_to_all | solution.py:53
  538.1 101.4 %all-to-all-start.15 = ((f32[32,1,6016]{2,1,0:T(1,128)}), f32[32,1,6016]{2,1,0:T(1,128)S(1)}, u32[]{:S(2)}, u32[]{:S(2)}) async-start(f32[32,1,6016]{2,1,0:T(1,128)} %broadcast_in_dim.58), calls=%async_computation.15 | async-start | bytes 1540096 | tf_op jit(solution)/shard_map/all_to_all | solution.py:55
  540.8 132.7 %all-reduce.42.cloned.1.call-start = ((), (), s32[]{:S(2)}) async-start(), calls=%async_computation.27 | async-start | bytes 1572864 | tf_op jit(solution)/shard_map/psum | solution.py:351
  544.7 91.8 %collective-permute-start.6 = (bf16[2,2,196,128]{3,2,1,0:T(8,128)(2,1)S(1)}, bf16[2,2,196,128]{3,2,1,0:T(8,128)(2,1)S(1)}, u32[]{:S(2)}, u32[]{:S(2)}) collective-permute-start(bf16[2,2,196,128]{3,2,1,0:T(8,128)(2,1)S(1)} %get-tuple-element.214), channel_id=1, source_target_pairs={{0,1},{1,2},{2,3},{3,4},{4,5},{5,6},{6,7},{8,9},{9,10},{10,11},{11... | collective-permute-start | bytes 602120 | tf_op jit(solution)/shard_map/ppermute | solution.py:22
  548.4 88.1 %collective-permute-start.7 = (bf16[2,2,196,128]{3,2,1,0:T(8,128)(2,1)S(1)}, bf16[2,2,196,128]{3,2,1,0:T(8,128)(2,1)S(1)}, u32[]{:S(2)}, u32[]{:S(2)}) collective-permute-start(bf16[2,2,196,128]{3,2,1,0:T(8,128)(2,1)S(1)} %get-tuple-element.215), channel_id=1, source_target_pairs={{1,0},{2,1},{3,2},{4,3},{5,4},{6,5},{7,6},{9,8},{10,9},{11,10},{12... | collective-permute-start | bytes 602120 | tf_op jit(solution)/shard_map/ppermute | solution.py:24
  555.6 81.1 %copy-start.3 = (f32[2,8,196,128]{3,2,1,0:T(8,128)S(1)}, f32[2,8,196,128]{3,2,1,0:T(8,128)}, u32[]{:S(2)}) copy-start(f32[2,8,196,128]{3,2,1,0:T(8,128)} %copy-done.2) | copy-start | bytes 4816900
  (107 other events, 639.1 us)
Sparse Core Ops, SparseCore 0:
  10.3 57.3 all-gather.3
  69.9 40.1 all-gather.5
  112.2 81.9 all-gather.7
  333.5 60.9 reduce-scatter.12
  398.3 94.3 reduce-scatter.14
  496.3 68.9 reduce-scatter.10
  569.1 67.2 reduce-scatter.8
  639.6 33.8 all-reduce.41
